TPU v7x, 32 devices: a whole 2x2x4 slice. The times are simulated.
32 devices in a mesh: blk: 8 (over z, x), col: 4 (over y, core).
Axes of the slice: x: 2, y: 2, z: 4, core: 2. Of those that a mesh axis runs over, the one named last changes fastest.
Arguments:
- points: float32 [16, 8192], P(None, 'blk'), may hold values from -5 to 5
- lengths: float32 [16], replicated, may hold values from 2 to 4
- noise: float32 [8192], P('blk'), may hold values from 0.5 to 2
- outscale: float32 [1], replicated, may hold values from 0.02 to 0.1
- solution: float32 [32, 8192], P('col', 'blk'), may hold values from -6 to 6
- residual: float32 [32, 8192], P('col', 'blk'), may hold values from -26 to 26
- direction: float32 [32, 8192], P('col', 'blk'), may hold values from -31 to 31
Outputs:
- solution_next: float32 [32, 8192], P('col', 'blk')
- residual_next: float32 [32, 8192], P('col', 'blk')
- direction_next: float32 [32, 8192], P('col', 'blk')
All inputs are finite; a program needn't handle non-finite values.
Results may differ from a plain program's by a relative error of at most 0.0003.
Values may be sent and summed in bfloat16 or wider, within the bound.
A program may use at most 64 MiB of HBM per device.

v0:
```python
import math

import jax
import jax.numpy as jnp
from jax import lax
from jax.sharding import PartitionSpec as P


def matern_tile(left, right, amplitude):
    cross = lax.dot_general(
        left,
        right,
        (((0,), (0,)), ((), ())),
        precision=lax.Precision.HIGHEST,
        preferred_element_type=jnp.float32,
    )
    left_sq = jnp.sum(left * left, axis=0)
    right_sq = jnp.sum(right * right, axis=0)
    dist_sq = jnp.maximum(left_sq[:, None] + right_sq[None, :] - 2.0 * cross, 0.0)
    radius = jnp.sqrt(5.0 * dist_sq)
    return (amplitude * (1.0 + radius + radius * radius / 3.0) * jnp.exp(-radius)).astype(
        jnp.bfloat16
    )


def local(points, lengths, noise, outscale, solution, residual, direction):
    amplitude = outscale[0]
    scaled = points / lengths[:, None]
    local_count = scaled.shape[1]
    lowered = direction.astype(jnp.bfloat16)
    norm_now = lax.psum(jnp.sum(residual * residual, axis=1), "blk")
    columns = lax.all_gather(lowered, "col", axis=0, tiled=True)
    row_count = local_count // lax.axis_size("col")
    offset_rows = lax.axis_index("col") * row_count
    rows_points = lax.dynamic_slice_in_dim(scaled, offset_rows, row_count, 1)
    column_count = columns.shape[0]
    every_columns = lax.all_gather(columns, "blk", axis=1, tiled=True)
    initial = jnp.zeros((column_count, row_count), jnp.float32)
    piece_points = lax.all_gather(scaled.astype(jnp.bfloat16), "blk", axis=1, tiled=True).astype(
        jnp.float32
    )
    block_width = math.gcd(piece_points.shape[1], 4096)
    block_count = piece_points.shape[1] // block_width

    def block_step(index_block, running):
        some_points = lax.dynamic_slice_in_dim(
            piece_points, index_block * block_width, block_width, 1
        )
        some_columns = lax.dynamic_slice_in_dim(
            every_columns, index_block * block_width, block_width, 1
        )
        kernel_tile = matern_tile(some_points, rows_points, amplitude)
        return running + jnp.dot(some_columns, kernel_tile, preferred_element_type=jnp.float32)

    direct = lax.fori_loop(0, block_count, block_step, initial)
    kernel_image = lax.all_to_all(direct, "col", split_axis=0, concat_axis=1, tiled=True)
    image = kernel_image + noise[None, :] * direction
    curve = lax.psum(jnp.sum(direction * image, axis=1), "blk")
    alpha = norm_now / curve
    solution_next = solution + alpha[:, None] * direction
    residual_next = residual - alpha[:, None] * image
    norm_next = lax.psum(jnp.sum(residual_next * residual_next, axis=1), "blk")
    direction_next = residual_next + (norm_next / norm_now)[:, None] * direction
    return (solution_next, residual_next, direction_next)


def solution(mesh):
    in_specs = (
        P(None, "blk"),
        P(),
        P("blk"),
        P(),
        P("col", "blk"),
        P("col", "blk"),
        P("col", "blk"),
    )
    out_specs = (P("col", "blk"), P("col", "blk"), P("col", "blk"))
    return jax.shard_map(local, mesh=mesh, in_specs=in_specs, out_specs=out_specs, check_vma=False)
```

profile of v0, /device:TPU:0, one launch (start us, length us, event | category | flops | bytes accessed | tf_op | source)
XLA Modules:
  0.0 136.3 jit_solution(16595515429106963590)
XLA Ops:
  0.6 0.9 fusion.8
  1.6 32.5 %all_gather.11 = bf16[16,8192]{1,0:T(8,128)(2,1)S(1)} all-gather(bf16[16,1024]{1,0:T(8,128)(2,1)S(1)} %get-tuple-element.202), channel_id=1, replica_groups=mesh['blk'=8,'col'=4] {'blk'}, dimensions={1}, use_global_device_ids=true | all-gather | bytes 294912 | tf_op jit(solution)/shard_map/all_gather | solution.py:39
  34.1 0.8 convert_element_type.18
  34.9 5.2 %all_gather.9 = bf16[32,1024]{1,0:T(8,128)(2,1)S(1)} all-gather(bf16[8,1024]{1,0:T(8,128)(2,1)S(1)} %convert_element_type.18), channel_id=1, replica_groups=mesh['blk'=8,'col'=4] {'col'}, dimensions={0}, use_global_device_ids=true | all-gather | bytes 81920 | tf_op jit(solution)/shard_map/all_gather | solution.py:32
  40.1 31.5 %all_gather.10 = bf16[32,8192]{1,0:T(8,128)(2,1)S(1)} all-gather(bf16[32,1024]{1,0:T(8,128)(2,1)S(1)} %all_gather.9), channel_id=1, replica_groups=mesh['blk'=8,'col'=4] {'blk'}, dimensions={1}, use_global_device_ids=true | all-gather | bytes 589824 | tf_op jit(solution)/shard_map/all_gather | solution.py:37
  71.7 0.0 copy-start
  71.7 0.0 copy-start.4
  71.7 0.0 copy-start.3
  71.7 17.5 %while.16 = (s32[]{:T(128)}, f32[32,256]{1,0:T(8,128)}, bf16[32,8192]{1,0:T(8,128)(2,1)S(1)}, f32[]{:T(128)}, f32[16,8192]{1,0:T(8,128)S(1)}, /*index=5*/f32[256...) while((s32[]{:T(128)}, f32[32,256]{1,0:T(8,128)}, ...), condition=%wide.region_5.0_spmd.clone, body=%wide.region_3.5_spmd.clone.sunk | while | flops 282210304 | bytes 5096629 | solution.py:55
  71.7 0.1 multiply_reduce_fusion.6
  71.8 7.2 %multiply_convert_fusion.2 = bf16[4096,256]{1,0:T(8,128)(2,1)S(1)} fusion(f32[16,256]{1,0:T(8,128)S(1)} %get-tuple-element.276, f32[256]{0:T(256)S(1)} %get-tuple-element.275, f32[4096]{0:T(1024)S(1)} %multiply_reduce_fusion.6, f32[]{:T(128)} %get-tuple-element.273, f32[16,8192]{1,0:T(8,128)S(1)} %get-tuple-element.274, s32[]{:T(128)S(6)} %select_n.16), kind=kOutput, calls=%fused_computation.5.clone.1 | convolution fusion | flops 214958080 | bytes 2393096 | tf_op jit(solution)/shard_map/while/body/eval_jaxpr/dot_general | solution.py:10
  79.0 1.1 convolution_add_fusion.2
  80.1 7.2 %multiply_convert_fusion.2 = bf16[4096,256]{1,0:T(8,128)(2,1)S(1)} fusion(f32[16,256]{1,0:T(8,128)S(1)} %get-tuple-element.276, f32[256]{0:T(256)S(1)} %get-tuple-element.275, f32[4096]{0:T(1024)S(1)} %multiply_reduce_fusion.6, f32[]{:T(128)} %get-tuple-element.273, f32[16,8192]{1,0:T(8,128)S(1)} %get-tuple-element.274, s32[]{:T(128)S(6)} %select_n.16), kind=kOutput, calls=%fused_computation.5.clone.1 | convolution fusion | flops 214958080 | bytes 2393096 | tf_op jit(solution)/shard_map/while/body/eval_jaxpr/dot_general | solution.py:10
  87.3 1.9 %convolution_add_fusion.2 = f32[32,256]{1,0:T(8,128)} fusion(bf16[4096,256]{1,0:T(8,128)(2,1)S(1)} %multiply_convert_fusion.2, bf16[32,8192]{1,0:T(8,128)(2,1)S(1)} %get-tuple-element.272, s32[]{:T(128)S(6)} %select_n.16, f32[32,256]{1,0:T(8,128)} %get-tuple-element.260, pred[]{:T(512)S(6)} %compare.3), kind=kOutput, calls=%fused_computation.6.clone.1 | convolution fusion | flops 67125248 | bytes 2424837 | tf_op jit(solution)/shard_map/while/body/eval_jaxpr/dot_general | solution.py:53
  89.2 3.3 %all-to-all-start = ((f32[4,8,256]{2,1,0:T(8,128)}), f32[4,8,256]{2,1,0:T(8,128)S(1)}, u32[]{:S(2)}, u32[]{:S(2)}) async-start(f32[4,8,256]{2,1,0:T(8,128)} %bitcast.1), calls=%async_computation | async-start | bytes 65536 | tf_op jit(solution)/shard_map/all_to_all | solution.py:56
  92.5 0.0 copy-done.2
  92.5 0.1 multiply_reduce_fusion.3
  92.6 3.8 %all-to-all-done = f32[4,8,256]{2,1,0:T(8,128)S(1)} async-done(((f32[4,8,256]{2,1,0:T(8,128)}), f32[4,8,256]{2,1,0:T(8,128)S(1)}, u32[]{:S(2)}, u32[]{:S(2)}) %all-to-all-start) | async-done | bytes 32800 | tf_op jit(solution)/shard_map/all_to_all | solution.py:56
  96.4 0.0 copy-done.4
  96.4 0.1 multiply_reduce_fusion.2
  96.5 21.1 %all-reduce = (f32[8]{0:T(128)S(1)}, f32[8]{0:T(128)S(1)}) all-reduce(f32[8]{0:T(128)S(1)} %multiply_reduce_fusion.3, f32[8]{0:T(128)S(1)} %multiply_reduce_fusion.2), channel_id=1, replica_groups=mesh['blk'=8,'col'=4] {'blk'}, use_global_device_ids=true, to_apply=%region_1.0 | all-reduce | flops 16 | bytes 128 | tf_op jit(solution)/shard_map/psum | solution.py:31
  117.7 0.8 multiply_reduce_fusion.1
  118.5 17.1 %psum.23 = f32[8]{0:T(128)S(1)} all-reduce(f32[8]{0:T(128)S(1)} %get-tuple-element.198), channel_id=1, replica_groups=mesh['blk'=8,'col'=4] {'blk'}, use_global_device_ids=true, to_apply=%region_9.0 | all-reduce | flops 8 | bytes 64 | tf_op jit(solution)/shard_map/psum | solution.py:62
  135.6 0.7 multiply_add_fusion
  (11 shorter events, 0.1 us)
Async XLA Ops:
  71.7 20.8 %copy-start.2 = (f32[8,1024]{1,0:T(8,128)S(1)}, f32[8,1024]{1,0:T(8,128)}, u32[]{:S(2)}) copy-start(f32[8,1024]{1,0:T(8,128)} %param.14) | copy-start | bytes 98308
  71.7 24.7 %copy-start = (f32[8,1024]{1,0:T(8,128)S(1)}, f32[8,1024]{1,0:T(8,128)}, u32[]{:S(2)}) copy-start(f32[8,1024]{1,0:T(8,128)} %param.15) | copy-start | bytes 98308
  71.7 24.7 %copy-start.4 = (f32[1024]{0:T(1024)S(1)}, f32[1024]{0:T(1024)}, u32[]{:S(2)}) copy-start(f32[1024]{0:T(1024)} %param.11) | copy-start | bytes 12292
  71.7 45.9 %copy-start.3 = (f32[8,1024]{1,0:T(8,128)S(1)}, f32[8,1024]{1,0:T(8,128)}, u32[]{:S(2)}) copy-start(f32[8,1024]{1,0:T(8,128)} %param.13) | copy-start | bytes 98308
  89.2 7.2 %all-to-all-start = ((f32[4,8,256]{2,1,0:T(8,128)}), f32[4,8,256]{2,1,0:T(8,128)S(1)}, u32[]{:S(2)}, u32[]{:S(2)}) async-start(f32[4,8,256]{2,1,0:T(8,128)} %bitcast.1), calls=%async_computation | async-start | bytes 65536 | tf_op jit(solution)/shard_map/all_to_all | solution.py:56
  118.5 17.8 %copy-start.1 = (f32[8,1024]{1,0:T(8,128)}, f32[8,1024]{1,0:T(8,128)S(1)}, u32[]{:S(2)}) copy-start(f32[8,1024]{1,0:T(8,128)S(1)} %get-tuple-element.199) | copy-start | bytes 98308
where the time goes:
time: 137 us; the launch traced here: 136 us
  blocking collectives  108 us (79%)
  matrix products  17.3 us (13%)
  waiting for transfers between devices  3.78 us (3%)
  other arithmetic  3.6 us (3%)
  starting transfers between devices  3.26 us (2%)
    all_gather x1, blocking collectives, local(): lax.all_gather(scaled.astype(jnp.bfloat16), 'blk', axis=1, tiled=True)  32.5 us
    all_gather x1, blocking collectives, local(): every_columns = lax.all_gather(columns, 'blk', axis=1, tiled=True)  31.5 us
    psum x1, blocking collectives, local(): norm_now = lax.psum(jnp.sum(residual * residual, axis=1), 'blk')  21.1 us
    psum x1, blocking collectives, local(): norm_next = lax.psum(jnp.sum(residual_next * residual_next, axis=1), 'blk')  17.1 us
    dot_general x2, matrix products, matern_tile(): lax.dot_general(left, right, (((0,), (0,)), ((), ())), precision=lax.Prec...  14.4 us
    all_gather x1, blocking collectives, local(): columns = lax.all_gather(lowered, 'col', axis=0, tiled=True)  5.23 us
    all_to_all x1, waiting for transfers between devices, local(): lax.all_to_all(direct, 'col', split_axis=0, concat_axis=1, tiled=True)  3.78 us
    all_to_all x1, starting transfers between devices, local(): lax.all_to_all(direct, 'col', split_axis=0, concat_axis=1, tiled=True)  3.26 us
  transfers between devices with their start and end apart: 1, of which 1 were waited for; matrix products, arithmetic and copies ran while one was open for 0% of the time, Pallas kernels for 0%

commit v1 on v0

v1 whole, which is shorter than its diff:
```python
import functools
import math

import jax
import jax.numpy as jnp
from jax import lax
from jax.experimental import pallas as pl
from jax.experimental.pallas import tpu as pltpu
from jax.sharding import PartitionSpec as P

MESH = pl.DeviceIdType.MESH
LOG2E = math.log2(math.e)
LN2 = math.log(2.0)
KAPPA = 5.0 * LOG2E * LOG2E
DEPTH = 64


def split3(x):
    first = x.astype(jnp.bfloat16).astype(jnp.float32)
    second = (x - first).astype(jnp.bfloat16).astype(jnp.float32)
    third = x - first - second
    return first, second, third


def extra_rows(rows, count):
    row = lax.broadcasted_iota(jnp.int32, (16, count), 0)
    block = jnp.zeros((16, count), jnp.float32)
    for index, value in enumerate(rows):
        block = jnp.where(row == index, value, block)
    return block.astype(jnp.bfloat16)


def kernel(
    nb, nc, tile,
    points, lengths, noise, outscale, solution, residual, direction,
    solution_next, residual_next, direction_next,
    low_own, pts_own, low_buf, pts_buf, far, near, kmat, part, part_in, stat, stat_in,
    low_send, low_recv, pts_send, pts_recv, part_send, part_recv, stat_send, stat_recv,
):
    b = lax.axis_index("blk")
    c = lax.axis_index("col")
    per = nb // nc
    dim, count = points.shape
    cols = direction.shape[0]
    half = count // 2
    tiles = count // tile
    quarter = b // per
    slot = b % per
    mine = quarter == c

    barrier = pltpu.get_barrier_semaphore()

    def greet(block, col):
        pl.semaphore_signal(barrier, inc=1, device_id=(block, col), device_id_type=MESH)

    def greet_sources(k, carry):
        block = c * per + k // nc
        col = k % nc

        @pl.when(jnp.logical_or(block != b, col != c))
        def _():
            greet(block, col)

        return carry

    lax.fori_loop(0, per * nc, greet_sources, 0)

    def greet_blocks(k, carry):
        greet((b + k) % nb, c)
        return carry

    lax.fori_loop(1, nb, greet_blocks, 0)
    for k in range(1, nc):
        greet(b, (c + k) % nc)

    row = lax.broadcasted_iota(jnp.int32, (dim, 128), 0)
    scale = jnp.zeros((dim, 128), jnp.float32)
    for k in range(dim):
        scale = jnp.where(row == k, lengths[k], scale)
    scaled = points[...] / scale[:, :1]
    pts_own[...] = scaled.astype(jnp.bfloat16)
    own = direction[...]
    low_own[...] = jnp.concatenate([own[:, :half], own[:, half:]], axis=0).astype(jnp.bfloat16)

    pl.semaphore_wait(
        barrier, nb - jnp.where(mine, 1, 0) + nb - 1 + nc - 1
    )

    def pts_copy(k):
        return pltpu.make_async_remote_copy(
            src_ref=pts_own, dst_ref=pts_buf.at[slot],
            send_sem=pts_send.at[k], recv_sem=pts_recv.at[slot],
            device_id=(k, quarter), device_id_type=MESH,
        )

    def low_copy(k):
        return pltpu.make_async_remote_copy(
            src_ref=low_own, dst_ref=low_buf.at[slot, c],
            send_sem=low_send.at[k], recv_sem=low_recv.at[slot, c],
            device_id=(k, quarter), device_id_type=MESH,
        )

    def each_pts(act):
        def step(k, carry):
            block = c + k * nc

            @pl.when(block != b)
            def _():
                act(pts_copy(block))

            return carry

        lax.fori_loop(0, per, step, 0)

    def each_low(act):
        def step(k, carry):
            block = (b + k) % nb

            @pl.when(jnp.logical_or(k != 0, jnp.logical_not(mine)))
            def _():
                act(low_copy(block))

            return carry

        lax.fori_loop(0, nb, step, 0)

    each_pts(lambda copy: copy.start())
    each_low(lambda copy: copy.start())

    @pl.when(mine)
    def _():
        pts_buf[slot] = pts_own[...]
        low_buf[slot, c] = low_own[...]

    first, second, third = split3(scaled * (-2.0 * KAPPA))
    norms = split3(KAPPA * jnp.sum(scaled * scaled, axis=0, keepdims=True))
    near[0:16, :] = first.astype(jnp.bfloat16)
    near[16:32, :] = second.astype(jnp.bfloat16)
    near[32:48, :] = third.astype(jnp.bfloat16)
    near[48:64, :] = extra_rows((1.0, 1.0, 1.0) + norms, count)

    amplitude = outscale[0]
    slope = amplitude * LN2
    bend = amplitude * (LN2 * LN2 / 3.0)

    def kernel_block(jb, carry):
        @pl.when(c * per + jb != b)
        def _():
            pltpu.make_async_copy(pts_buf.at[jb], pts_buf.at[jb], pts_recv.at[jb]).wait()

        other = pts_buf[jb]
        wide = other.astype(jnp.float32)
        squares = split3(KAPPA * jnp.sum(wide * wide, axis=0, keepdims=True))
        stacked = jnp.concatenate(
            [other, other, other, extra_rows(squares + (1.0, 1.0, 1.0), count)], axis=0
        )
        far[...] = stacked.T

        def kernel_tile(it, inner):
            cut = pl.ds(pl.multiple_of(it * tile, tile), tile)
            gap = jnp.dot(far[...], near[:, cut], preferred_element_type=jnp.float32)
            gap = jnp.maximum(gap, 1e-30)
            radius = gap * lax.rsqrt(gap)
            value = (amplitude + radius * (slope + radius * bend)) * jnp.exp2(-radius)
            kmat[jb, :, cut] = value.astype(jnp.bfloat16)
            return inner

        return lax.fori_loop(0, tiles, kernel_tile, carry)

    lax.fori_loop(0, per, kernel_block, 0)

    def wait_low(k, carry):
        jb = k // nc
        col = k % nc

        @pl.when(jnp.logical_or(c * per + jb != b, col != c))
        def _():
            pltpu.make_async_copy(
                low_buf.at[jb, col], low_buf.at[jb, col], low_recv.at[jb, col]
            ).wait()

        return carry

    lax.fori_loop(0, per * nc, wait_low, 0)

    def part_copy(it, col):
        cut = pl.ds(pl.multiple_of(it * tile, tile), tile)
        return pltpu.make_async_remote_copy(
            src_ref=part.at[col, :, cut], dst_ref=part_in.at[c, :, cut],
            send_sem=part_send.at[it, col], recv_sem=part_recv.at[it, c],
            device_id=(b, col), device_id_type=MESH,
        )

    def image_tile(it, carry):
        cut = pl.ds(pl.multiple_of(it * tile, tile), tile)

        def image_block(jb, total):
            shards = []
            for col in range(nc):
                wide = low_buf[jb, col].astype(jnp.float32)
                shards.append(jnp.concatenate([wide[:cols], wide[cols:]], axis=1))
            low = jnp.concatenate(shards, axis=0).astype(jnp.bfloat16)
            return total + jnp.dot(low, kmat[jb, :, cut], preferred_element_type=jnp.float32)

        total = lax.fori_loop(0, per, image_block, jnp.zeros((nc * cols, tile), jnp.float32))
        for col in range(nc):
            part[col, :, cut] = total[col * cols : (col + 1) * cols]
        for k in range(1, nc):
            part_copy(it, (c + k) % nc).start()
        return carry

    lax.fori_loop(0, tiles, image_tile, 0)

    now = residual[...]
    image = part[c] + noise[...] * own
    for k in range(1, nc):
        col = (c + k) % nc
        for it in range(tiles):
            cut = pl.ds(it * tile, tile)
            pltpu.make_async_copy(
                part_in.at[col, :, cut], part_in.at[col, :, cut], part_recv.at[it, col]
            ).wait()
        image = image + part_in[col]

    lane = lax.broadcasted_iota(jnp.int32, (cols, 128), 1)
    sums = jnp.zeros((cols, 128), jnp.float32)
    for index, product in enumerate((own * image, now * image, image * image, now * now)):
        sums = jnp.where(lane == index, jnp.sum(product, axis=1, keepdims=True), sums)
    stat[...] = sums

    def stat_copy(block):
        return pltpu.make_async_remote_copy(
            src_ref=stat, dst_ref=stat_in.at[b],
            send_sem=stat_send.at[block], recv_sem=stat_recv.at[b],
            device_id=(block, c), device_id_type=MESH,
        )

    def start_stat(k, carry):
        stat_copy((b + k) % nb).start()
        return carry

    lax.fori_loop(1, nb, start_stat, 0)

    def add_stat(k, total):
        block = (b + k) % nb
        pltpu.make_async_copy(stat_in.at[block], stat_in.at[block], stat_recv.at[block]).wait()
        return total + stat_in[block]

    sums = lax.fori_loop(1, nb, add_stat, sums)
    curve, mixed, power, norm_now = (sums[:, index : index + 1] for index in range(4))
    alpha = norm_now / curve
    norm_next = norm_now - 2.0 * alpha * mixed + alpha * alpha * power
    after = now - alpha * image
    solution_next[...] = solution[...] + alpha * own
    residual_next[...] = after
    direction_next[...] = after + (norm_next / norm_now) * own

    each_pts(lambda copy: copy.wait_send())
    each_low(lambda copy: copy.wait_send())

    def sent_part(k, carry):
        part_copy(k // (nc - 1), (c + 1 + k % (nc - 1)) % nc).wait_send()
        return carry

    lax.fori_loop(0, tiles * (nc - 1), sent_part, 0)

    def sent_stat(k, carry):
        stat_copy((b + k) % nb).wait_send()
        return carry

    lax.fori_loop(1, nb, sent_stat, 0)


def local(nb, nc, points, lengths, noise, outscale, solution, residual, direction):
    dim, count = points.shape
    cols = direction.shape[0]
    per = nb // nc
    tile = math.gcd(count, 256)
    tiles = count // tile
    vmem = pl.BlockSpec(memory_space=pltpu.VMEM)
    smem = pl.BlockSpec(memory_space=pltpu.SMEM)
    state = jax.ShapeDtypeStruct((cols, count), jnp.float32)
    dma = pltpu.SemaphoreType.DMA
    entries = per * count * count
    return pl.pallas_call(
        functools.partial(kernel, nb, nc, tile),
        out_shape=(state, state, state),
        in_specs=[vmem, smem, vmem, smem, vmem, vmem, vmem],
        out_specs=(vmem, vmem, vmem),
        scratch_shapes=[
            pltpu.VMEM((2 * cols, count // 2), jnp.bfloat16),
            pltpu.VMEM((dim, count), jnp.bfloat16),
            pltpu.VMEM((per, nc, 2 * cols, count // 2), jnp.bfloat16),
            pltpu.VMEM((per, dim, count), jnp.bfloat16),
            pltpu.VMEM((count, DEPTH), jnp.bfloat16),
            pltpu.VMEM((DEPTH, count), jnp.bfloat16),
            pltpu.VMEM((per, count, count), jnp.bfloat16),
            pltpu.VMEM((nc, cols, count), jnp.float32),
            pltpu.VMEM((nc, cols, count), jnp.float32),
            pltpu.VMEM((cols, 128), jnp.float32),
            pltpu.VMEM((nb, cols, 128), jnp.float32),
            dma((nb,)), dma((per, nc)), dma((nb,)), dma((per,)),
            dma((tiles, nc)), dma((tiles, nc)), dma((nb,)), dma((nb,)),
        ],
        compiler_params=pltpu.CompilerParams(
            collective_id=0, has_side_effects=True, vmem_limit_bytes=56 * 1024 * 1024
        ),
        cost_estimate=pl.CostEstimate(
            flops=2 * entries * (DEPTH + nc * cols), bytes_accessed=1 << 19, transcendentals=2 * entries
        ),
    )(points, lengths, noise.reshape(1, count), outscale, solution, residual, direction)


def solution(mesh):
    in_specs = (
        P(None, "blk"), P(), P("blk"), P(),
        P("col", "blk"), P("col", "blk"), P("col", "blk"),
    )
    out_specs = (P("col", "blk"), P("col", "blk"), P("col", "blk"))
    body = functools.partial(local, mesh.shape["blk"], mesh.shape["col"])
    return jax.shard_map(body, mesh=mesh, in_specs=in_specs, out_specs=out_specs, check_vma=False)
```

time: 137 us -> 30.5 us (0.22)
  blocking collectives: 108 us -> 0 us
  Pallas kernels: 0 us -> 26.1 us
  matrix products: 17.3 us -> 0 us
  waiting for transfers between devices: 3.78 us -> 0 us
  other arithmetic: 3.6 us -> 0 us
  starting transfers between devices: 3.26 us -> 0 us
  local copies, waits for them, and re-layouts: 0.03 us -> 2.77 us
    all_gather x3 -> x0, blocking collectives: 69.3 us -> none  [the longest x1 32.5 us: local(): lax.all_gather(scaled.astype(jnp.bfloat16), 'blk', axis=1, tiled=True)]
    psum x2 -> x0, blocking collectives: 38.3 us -> none  [the longest x1 21.1 us: local(): norm_now = lax.psum(jnp.sum(residual * residual, axis=1), 'blk')]
    pallas_call x0 -> x1, Pallas kernels: none -> 26.1 us  [local(): pl.pallas_call(functools.partial(kernel, nb, nc, tile), out_shape=(state,...]
    dot_general x4 -> x0, matrix products: 17.3 us -> none  [the longest x2 14.4 us: matern_tile(): lax.dot_general(left, right, (((0,), (0,)), ((), ())), precision=lax.Prec...]
    all_to_all x1 -> x0, waiting for transfers between devices: 3.78 us -> none  [local(): lax.all_to_all(direct, 'col', split_axis=0, concat_axis=1, tiled=True)]
    all_to_all x1 -> x0, starting transfers between devices: 3.26 us -> none  [local(): lax.all_to_all(direct, 'col', split_axis=0, concat_axis=1, tiled=True)]
    unnamed x10 -> x7, local copies, waits for them, and re-layouts: 0.03 us -> 2.77 us
    convert_element_type x3 -> x0, other arithmetic: 1.72 us -> none  [the longest x1 0.92 us: local(): scaled.astype(jnp.bfloat16)]
  transfers between devices with their start and end apart: 1 -> 0, of which waited for: 1 -> 0; matrix products, arithmetic and copies ran while one was open for 0% -> 0% of each run, Pallas kernels for 0% -> 0%
where the time goes in v1:
time: 30.5 us; the launch traced here: 30.2 us
  Pallas kernels  26.1 us (86%)
  local copies, waits for them, and re-layouts  2.77 us (9%)
  between operations  1.3 us (4%)
    pallas_call x1, Pallas kernels, local(): pl.pallas_call(functools.partial(kernel, nb, nc, tile), out_shape=(state,...  26.1 us
    unnamed x7, local copies, waits for them, and re-layouts  2.77 us

profile of v1, /device:TPU:0, one launch (start us, length us, event | category | flops | bytes accessed | tf_op | source)
XLA Modules:
  0.0 30.2 jit_solution(8740983312252748133)
XLA Ops:
  1.3 26.1 %shard_map.94 = (f32[8,1024]{1,0:T(8,128)}, f32[8,1024]{1,0:T(8,128)}, f32[8,1024]{1,0:T(8,128)}) custom-call(f32[16,1024]{1,0:T(8,128)} %points.1, f32[16]{0:T(128)} %lengths.1, f32[1,1024]{1,0:T(1,128)} %bitcast.1, f32[1]{0:T(128)S(6)} %copy.13.outscale, f32[8,1024]{1,0:T(8,128)} %solution.1, f32[8,1024]{1,0:T(8,128)} %residual.1, f32[8,1024]{1,0:T(8,128)} %direction.1), custom_call_target="tpu_custom_call" | custom-call | flops 402653184 | bytes 524288 | tf_op jit(solution)/shard_map/pallas_call | solution.py:285
  27.4 0.0 copy-start.1
  27.4 1.4 %copy.14 = f32[8,1024]{1,0:T(8,128)} copy(f32[8,1024]{1,0:T(8,128)} %get-tuple-element.6) | data formatting | bytes 65536
  28.8 0.0 copy-done.1
  28.8 0.0 copy-start
  28.8 0.6 %copy.15 = f32[8,1024]{1,0:T(8,128)} copy(f32[8,1024]{1,0:T(8,128)S(1)} %copy-done.1) | data formatting | bytes 65536
  29.4 0.2 copy-done
  29.6 0.6 %copy.16 = f32[8,1024]{1,0:T(8,128)} copy(f32[8,1024]{1,0:T(8,128)S(1)} %copy-done) | data formatting | bytes 65536
Async XLA Ops:
  27.4 1.4 %copy-start.1 = (f32[8,1024]{1,0:T(8,128)S(1)}, f32[8,1024]{1,0:T(8,128)}, u32[]{:S(2)}) copy-start(f32[8,1024]{1,0:T(8,128)} %get-tuple-element.7) | copy-start | bytes 98308
  28.8 0.8 %copy-start = (f32[8,1024]{1,0:T(8,128)S(1)}, f32[8,1024]{1,0:T(8,128)}, u32[]{:S(2)}) copy-start(f32[8,1024]{1,0:T(8,128)} %get-tuple-element.8) | copy-start | bytes 98308

commit v2 on v1

--- a/solution.py
+++ b/solution.py
@@ -32,8 +32,9 @@
 
 def kernel(
     nb, nc, tile,
-    points, lengths, noise, outscale, solution, residual, direction,
-    solution_next, residual_next, direction_next,
+    points_in, lengths_in, noise_in, outscale_in, residual_in, direction_in,
+    image_out, sums_out,
+    points, lengths, noise, outscale, residual, direction, in_sems,
     low_own, pts_own, low_buf, pts_buf, far, near, kmat, part, part_in, stat, stat_in,
     low_send, low_recv, pts_send, pts_recv, part_send, part_recv, stat_send, stat_recv,
 ):
@@ -48,6 +49,18 @@
     slot = b % per
     mine = quarter == c
 
+    loads = [
+        pltpu.make_async_copy(source, target, in_sems.at[index])
+        for index, (source, target) in enumerate(
+            (
+                (points_in, points), (lengths_in, lengths), (direction_in, direction),
+                (noise_in, noise), (outscale_in, outscale), (residual_in, residual),
+            )
+        )
+    ]
+    for load in loads:
+        load.start()
+
     barrier = pltpu.get_barrier_semaphore()
 
     def greet(block, col):
@@ -73,6 +86,8 @@
     for k in range(1, nc):
         greet(b, (c + k) % nc)
 
+    for load in loads:
+        load.wait()
     row = lax.broadcasted_iota(jnp.int32, (dim, 128), 0)
     scale = jnp.zeros((dim, 128), jnp.float32)
     for k in range(dim):
@@ -139,7 +154,7 @@
     near[32:48, :] = third.astype(jnp.bfloat16)
     near[48:64, :] = extra_rows((1.0, 1.0, 1.0) + norms, count)
 
-    amplitude = outscale[0]
+    amplitude = outscale[...]
     slope = amplitude * LN2
     bend = amplitude * (LN2 * LN2 / 3.0)
 
@@ -247,13 +262,8 @@
         return total + stat_in[block]
 
     sums = lax.fori_loop(1, nb, add_stat, sums)
-    curve, mixed, power, norm_now = (sums[:, index : index + 1] for index in range(4))
-    alpha = norm_now / curve
-    norm_next = norm_now - 2.0 * alpha * mixed + alpha * alpha * power
-    after = now - alpha * image
-    solution_next[...] = solution[...] + alpha * own
-    residual_next[...] = after
-    direction_next[...] = after + (norm_next / norm_now) * own
+    image_out[...] = image
+    sums_out[...] = sums
 
     each_pts(lambda copy: copy.wait_send())
     each_low(lambda copy: copy.wait_send())
@@ -278,16 +288,24 @@
     tile = math.gcd(count, 256)
     tiles = count // tile
     vmem = pl.BlockSpec(memory_space=pltpu.VMEM)
-    smem = pl.BlockSpec(memory_space=pltpu.SMEM)
     state = jax.ShapeDtypeStruct((cols, count), jnp.float32)
+    totals = jax.ShapeDtypeStruct((cols, 128), jnp.float32)
+    here = pl.BlockSpec(memory_space=pl.ANY)
     dma = pltpu.SemaphoreType.DMA
     entries = per * count * count
-    return pl.pallas_call(
+    image, sums = pl.pallas_call(
         functools.partial(kernel, nb, nc, tile),
-        out_shape=(state, state, state),
-        in_specs=[vmem, smem, vmem, smem, vmem, vmem, vmem],
-        out_specs=(vmem, vmem, vmem),
+        out_shape=(state, totals),
+        in_specs=[here] * 6,
+        out_specs=(vmem, vmem),
         scratch_shapes=[
+            pltpu.VMEM((dim, count), jnp.float32),
+            pltpu.SMEM((dim,), jnp.float32),
+            pltpu.VMEM((1, count), jnp.float32),
+            pltpu.VMEM((1, 1), jnp.float32),
+            pltpu.VMEM((cols, count), jnp.float32),
+            pltpu.VMEM((cols, count), jnp.float32),
+            dma((6,)),
             pltpu.VMEM((2 * cols, count // 2), jnp.bfloat16),
             pltpu.VMEM((dim, count), jnp.bfloat16),
             pltpu.VMEM((per, nc, 2 * cols, count // 2), jnp.bfloat16),
@@ -308,7 +326,16 @@
         cost_estimate=pl.CostEstimate(
             flops=2 * entries * (DEPTH + nc * cols), bytes_accessed=1 << 19, transcendentals=2 * entries
         ),
-    )(points, lengths, noise.reshape(1, count), outscale, solution, residual, direction)
+    )(points, lengths, noise.reshape(1, count), outscale.reshape(1, 1), residual, direction)
+    curve, mixed, power, norm_now = (sums[:, index : index + 1] for index in range(4))
+    alpha = norm_now / curve
+    norm_next = norm_now - 2.0 * alpha * mixed + alpha * alpha * power
+    after = residual - alpha * image
+    return (
+        solution + alpha * direction,
+        after,
+        after + (norm_next / norm_now) * direction,
+    )
 
 
 def solution(mesh):

time: 30.5 us -> 29.3 us (0.961)
  local copies, waits for them, and re-layouts: 2.77 us -> 0.01 us
  other arithmetic: 0 us -> 2.52 us
  Pallas kernels: 26.1 us -> 25.1 us
    unnamed x7 -> x6, local copies, waits for them, and re-layouts: 2.77 us -> 0.01 us
    add x0 -> x1, other arithmetic: none -> 1.47 us  [local(): after + norm_next / norm_now * direction]
    div x0 -> x1, other arithmetic: none -> 1.05 us  [local(): norm_next / norm_now]
    pallas_call x1, Pallas kernels: 26.1 us -> 25.1 us  [local(): pl.pallas_call(functools.partial(kernel, nb, nc, tile), out_shape=(state,...]
where the time goes in v2:
time: 29.3 us; the launch traced here: 29 us
  Pallas kernels  25.1 us (86%)
  other arithmetic  2.52 us (9%)
  between operations  1.33 us (5%)
    pallas_call x1, Pallas kernels, local(): pl.pallas_call(functools.partial(kernel, nb, nc, tile), out_shape=(state,...  25.1 us
    add x1, other arithmetic, local(): after + norm_next / norm_now * direction  1.47 us
    div x1, other arithmetic, local(): norm_next / norm_now  1.05 us

profile of v2, /device:TPU:0, one launch (start us, length us, event | category | flops | bytes accessed | tf_op | source)
XLA Modules:
  0.0 29.0 jit_solution(5506477674005293936)
XLA Ops:
  1.3 0.0 copy-start
  1.3 0.0 copy-start.1
  1.3 0.0 copy-start.2
  1.3 25.1 %shard_map.94 = (f32[8,1024]{1,0:T(8,128)}, f32[8,128]{1,0:T(8,128)}) custom-call(f32[16,1024]{1,0:T(8,128)} %points_in.1, f32[16]{0:T(128)} %lengths_in.1, f32[1,1024]{1,0:T(1,128)} %bitcast.3, f32[1,1]{1,0:T(1,128)} %bitcast.2.outscale_in, f32[8,1024]{1,0:T(8,128)} %residual_in.1, f32[8,1024]{1,0:T(8,128)} %direction_in.1), custom_call_target="tpu_custom_call" | custom-call | flops 402653184 | bytes 524288 | tf_op jit(solution)/shard_map/pallas_call | solution.py:296
  26.5 1.0 %divide_reduce_fusion = (f32[8]{0:T(128)S(1)}, f32[8]{0:T(128)S(1)}) fusion(f32[8,128]{1,0:T(8,128)} %get-tuple-element.5), kind=kLoop, calls=%fused_computation.3 | loop fusion | flops 64 | bytes 192 | tf_op jit(solution)/shard_map/div | solution.py:337
  27.5 0.0 copy-done
  27.5 0.0 copy-done.1
  27.5 0.0 copy-done.2
  27.5 1.5 %multiply_add_fusion = (f32[8,1024]{1,0:T(8,128)}, f32[8,1024]{1,0:T(8,128)}, f32[8,1024]{1,0:T(8,128)}) fusion(f32[8,1024]{1,0:T(8,128)S(1)} %copy-done, f32[8]{0:T(128)S(1)} %get-tuple-element.7, f32[8,1024]{1,0:T(8,128)S(1)} %copy-done.1, f32[8,1024]{1,0:T(8,128)} %get-tuple-element.6, f32[8]{0:T(128)S(1)} %get-tuple-element.8, f32[8,1024]{1,0:T(8,128)S(1)} %copy-done.2), kind=kLoop, calls=%fused_computation | loop fusion | flops 49152 | bytes 229440 | tf_op jit(solution)/shard_map/add | solution.py:337
Async XLA Ops:
  1.3 26.2 %copy-start = (f32[8,1024]{1,0:T(8,128)S(1)}, f32[8,1024]{1,0:T(8,128)}, u32[]{:S(2)}) copy-start(f32[8,1024]{1,0:T(8,128)} %direction_in.1) | copy-start | bytes 98308
  1.3 26.2 %copy-start.1 = (f32[8,1024]{1,0:T(8,128)S(1)}, f32[8,1024]{1,0:T(8,128)}, u32[]{:S(2)}) copy-start(f32[8,1024]{1,0:T(8,128)} %residual_in.1) | copy-start | bytes 98308
  1.3 26.2 %copy-start.2 = (f32[8,1024]{1,0:T(8,128)S(1)}, f32[8,1024]{1,0:T(8,128)}, u32[]{:S(2)}) copy-start(f32[8,1024]{1,0:T(8,128)} %param.11) | copy-start | bytes 98308

commit v3 on v2

--- a/solution.py
+++ b/solution.py
@@ -33,9 +33,9 @@
 def kernel(
     nb, nc, tile,
     points_in, lengths_in, noise_in, outscale_in, residual_in, direction_in,
-    image_out, sums_out,
+    step_out, drop_out, keep_out,
     points, lengths, noise, outscale, residual, direction, in_sems,
-    low_own, pts_own, low_buf, pts_buf, far, near, kmat, part, part_in, stat, stat_in,
+    low_own, pts_own, low_buf, pts_buf, far, near, low_all, kmat_a, kmat_b, part, part_in, stat, stat_in,
     low_send, low_recv, pts_send, pts_recv, part_send, part_recv, stat_send, stat_recv,
 ):
     b = lax.axis_index("blk")
@@ -154,11 +154,9 @@
     near[32:48, :] = third.astype(jnp.bfloat16)
     near[48:64, :] = extra_rows((1.0, 1.0, 1.0) + norms, count)
 
-    amplitude = outscale[...]
-    slope = amplitude * LN2
-    bend = amplitude * (LN2 * LN2 / 3.0)
-
-    def kernel_block(jb, carry):
+    shift = jnp.log(outscale[...] * (LN2 * LN2 / 3.0)) * LOG2E
+
+    def form(jb):
         @pl.when(c * per + jb != b)
         def _():
             pltpu.make_async_copy(pts_buf.at[jb], pts_buf.at[jb], pts_recv.at[jb]).wait()
@@ -171,32 +169,54 @@
         )
         far[...] = stacked.T
 
-        def kernel_tile(it, inner):
-            cut = pl.ds(pl.multiple_of(it * tile, tile), tile)
-            gap = jnp.dot(far[...], near[:, cut], preferred_element_type=jnp.float32)
-            gap = jnp.maximum(gap, 1e-30)
-            radius = gap * lax.rsqrt(gap)
-            value = (amplitude + radius * (slope + radius * bend)) * jnp.exp2(-radius)
-            kmat[jb, :, cut] = value.astype(jnp.bfloat16)
-            return inner
-
-        return lax.fori_loop(0, tiles, kernel_tile, carry)
-
-    lax.fori_loop(0, per, kernel_block, 0)
-
-    def wait_low(k, carry):
-        jb = k // nc
-        col = k % nc
-
-        @pl.when(jnp.logical_or(c * per + jb != b, col != c))
-        def _():
-            pltpu.make_async_copy(
-                low_buf.at[jb, col], low_buf.at[jb, col], low_recv.at[jb, col]
-            ).wait()
-
-        return carry
-
-    lax.fori_loop(0, per * nc, wait_low, 0)
+    def fill(it, kmat):
+        cut = slice(it * tile, (it + 1) * tile)
+        gap = jnp.dot(far[...], near[:, cut], preferred_element_type=jnp.float32)
+        gap = jnp.maximum(gap, 1e-30)
+        radius = gap * lax.rsqrt(gap)
+        value = ((radius + 3.0 / LN2) * radius + 3.0 / (LN2 * LN2)) * jnp.exp2(shift - radius)
+        kmat[:, cut] = value.astype(jnp.bfloat16)
+
+    def wait_low(jb):
+        for col in range(nc):
+            @pl.when(jnp.logical_or(c * per + jb != b, c != col))
+            def _():
+                pltpu.make_async_copy(
+                    low_buf.at[jb, col], low_buf.at[jb, col], low_recv.at[jb, col]
+                ).wait()
+
+        shards = []
+        for col in range(nc):
+            wide = low_buf[jb, col].astype(jnp.float32)
+            shards.append(jnp.concatenate([wide[:cols], wide[cols:]], axis=1))
+        low_all[...] = jnp.concatenate(shards, axis=0).astype(jnp.bfloat16)
+
+    def add_image(it, kmat, first):
+        cut = slice(it * tile, (it + 1) * tile)
+        total = jnp.dot(low_all[...], kmat[:, cut], preferred_element_type=jnp.float32)
+        for col in range(nc):
+            rows = total[col * cols : (col + 1) * cols]
+            part[col, :, cut] = rows if first else part[col, :, cut] + rows
+
+    def both(jb, now_mat, last_mat, first):
+        form(jb)
+        wait_low(jb - 1)
+        for it in range(tiles):
+            fill(it, now_mat)
+            add_image(it, last_mat, first)
+
+    form(0)
+    for it in range(tiles):
+        fill(it, kmat_a)
+    both(1, kmat_b, kmat_a, True)
+
+    def pair(p, carry):
+        both(2 * p, kmat_a, kmat_b, False)
+        both(2 * p + 1, kmat_b, kmat_a, False)
+        return carry
+
+    if per > 2:
+        lax.fori_loop(1, per // 2, pair, 0)
 
     def part_copy(it, col):
         cut = pl.ds(pl.multiple_of(it * tile, tile), tile)
@@ -206,25 +226,11 @@
             device_id=(b, col), device_id_type=MESH,
         )
 
-    def image_tile(it, carry):
-        cut = pl.ds(pl.multiple_of(it * tile, tile), tile)
-
-        def image_block(jb, total):
-            shards = []
-            for col in range(nc):
-                wide = low_buf[jb, col].astype(jnp.float32)
-                shards.append(jnp.concatenate([wide[:cols], wide[cols:]], axis=1))
-            low = jnp.concatenate(shards, axis=0).astype(jnp.bfloat16)
-            return total + jnp.dot(low, kmat[jb, :, cut], preferred_element_type=jnp.float32)
-
-        total = lax.fori_loop(0, per, image_block, jnp.zeros((nc * cols, tile), jnp.float32))
-        for col in range(nc):
-            part[col, :, cut] = total[col * cols : (col + 1) * cols]
+    wait_low(per - 1)
+    for it in range(tiles):
+        add_image(it, kmat_b, False)
         for k in range(1, nc):
             part_copy(it, (c + k) % nc).start()
-        return carry
-
-    lax.fori_loop(0, tiles, image_tile, 0)
 
     now = residual[...]
     image = part[c] + noise[...] * own
@@ -262,8 +268,12 @@
         return total + stat_in[block]
 
     sums = lax.fori_loop(1, nb, add_stat, sums)
-    image_out[...] = image
-    sums_out[...] = sums
+    curve, mixed, power, norm_now = (sums[:, index : index + 1] for index in range(4))
+    alpha = norm_now / curve
+    norm_next = norm_now - 2.0 * alpha * mixed + alpha * alpha * power
+    step_out[...] = alpha * own
+    drop_out[...] = alpha * image
+    keep_out[...] = (norm_next / norm_now) * own
 
     each_pts(lambda copy: copy.wait_send())
     each_low(lambda copy: copy.wait_send())
@@ -289,15 +299,14 @@
     tiles = count // tile
     vmem = pl.BlockSpec(memory_space=pltpu.VMEM)
     state = jax.ShapeDtypeStruct((cols, count), jnp.float32)
-    totals = jax.ShapeDtypeStruct((cols, 128), jnp.float32)
     here = pl.BlockSpec(memory_space=pl.ANY)
     dma = pltpu.SemaphoreType.DMA
     entries = per * count * count
-    image, sums = pl.pallas_call(
+    step, drop, keep = pl.pallas_call(
         functools.partial(kernel, nb, nc, tile),
-        out_shape=(state, totals),
+        out_shape=(state, state, state),
         in_specs=[here] * 6,
-        out_specs=(vmem, vmem),
+        out_specs=(vmem, vmem, vmem),
         scratch_shapes=[
             pltpu.VMEM((dim, count), jnp.float32),
             pltpu.SMEM((dim,), jnp.float32),
@@ -312,7 +321,9 @@
             pltpu.VMEM((per, dim, count), jnp.bfloat16),
             pltpu.VMEM((count, DEPTH), jnp.bfloat16),
             pltpu.VMEM((DEPTH, count), jnp.bfloat16),
-            pltpu.VMEM((per, count, count), jnp.bfloat16),
+            pltpu.VMEM((nc * cols, count), jnp.bfloat16),
+            pltpu.VMEM((count, count), jnp.bfloat16),
+            pltpu.VMEM((count, count), jnp.bfloat16),
             pltpu.VMEM((nc, cols, count), jnp.float32),
             pltpu.VMEM((nc, cols, count), jnp.float32),
             pltpu.VMEM((cols, 128), jnp.float32),
@@ -327,15 +338,8 @@
             flops=2 * entries * (DEPTH + nc * cols), bytes_accessed=1 << 19, transcendentals=2 * entries
         ),
     )(points, lengths, noise.reshape(1, count), outscale.reshape(1, 1), residual, direction)
-    curve, mixed, power, norm_now = (sums[:, index : index + 1] for index in range(4))
-    alpha = norm_now / curve
-    norm_next = norm_now - 2.0 * alpha * mixed + alpha * alpha * power
-    after = residual - alpha * image
-    return (
-        solution + alpha * direction,
-        after,
-        after + (norm_next / norm_now) * direction,
-    )
+    after = residual - drop
+    return (solution + step, after, after + keep)
 
 
 def solution(mesh):

time: 29.3 us -> 27 us (0.922)
  Pallas kernels: 25.1 us -> 23.4 us
  other arithmetic: 2.52 us -> 2.03 us
    pallas_call x1, Pallas kernels: 25.1 us -> 23.4 us  [local(): pl.pallas_call(functools.partial(kernel, nb, nc, tile), out_shape=(state,...]
    div x1 -> x0, other arithmetic: 1.05 us -> none  [local(): norm_next / norm_now]
    add x1 -> x2, other arithmetic: 1.47 us -> 2.03 us  [local(): return (solution + step, after, after + keep)]
where the time goes in v3:
time: 27 us; the launch traced here: 26.8 us
  Pallas kernels  23.4 us (87%)
  other arithmetic  2.03 us (8%)
  between operations  1.33 us (5%)
    pallas_call x1, Pallas kernels, local(): pl.pallas_call(functools.partial(kernel, nb, nc, tile), out_shape=(state,...  23.4 us
    add x2, other arithmetic, local(): return (solution + step, after, after + keep)  2.03 us

profile of v3, /device:TPU:0, one launch (start us, length us, event | category | flops | bytes accessed | tf_op | source)
XLA Modules:
  0.0 26.8 jit_solution(3818716896683873939)
XLA Ops:
  1.3 0.0 copy-start
  1.3 23.4 %shard_map.94 = (f32[8,1024]{1,0:T(8,128)}, f32[8,1024]{1,0:T(8,128)}, f32[8,1024]{1,0:T(8,128)}) custom-call(f32[16,1024]{1,0:T(8,128)} %points_in.1, f32[16]{0:T(128)} %lengths_in.1, f32[1,1024]{1,0:T(1,128)} %bitcast.3, f32[1,1]{1,0:T(1,128)} %bitcast.2.outscale_in, f32[8,1024]{1,0:T(8,128)} %residual_in.1, f32[8,1024]{1,0:T(8,128)} %direction_in.1), custom_call_target="tpu_custom_call" | custom-call | flops 402653184 | bytes 524288 | tf_op jit(solution)/shard_map/pallas_call | solution.py:305
  24.7 0.0 copy-done
  24.7 0.0 copy-start.1
  24.7 0.0 copy-start.2
  24.7 0.0 copy-start.3
  24.7 1.4 %add.6 = f32[8,1024]{1,0:T(8,128)} add(f32[8,1024]{1,0:T(8,128)S(1)} %copy-done, f32[8,1024]{1,0:T(8,128)} %get-tuple-element.6) | non-fusion elementwise | flops 8192 | bytes 98304 | tf_op jit(solution)/shard_map/add | solution.py:342
  26.1 0.0 copy-done.1
  26.1 0.0 copy-done.2
  26.1 0.0 copy-done.3
  26.1 0.6 %fusion = (f32[8,1024]{1,0:T(8,128)}, f32[8,1024]{1,0:T(8,128)}) fusion(f32[8,1024]{1,0:T(8,128)S(1)} %copy-done.3, f32[8,1024]{1,0:T(8,128)S(1)} %copy-done.1, f32[8,1024]{1,0:T(8,128)S(1)} %copy-done.2), kind=kLoop, calls=%fused_computation | loop fusion | flops 16384 | bytes 163840 | tf_op jit(solution)/shard_map/add | solution.py:342
Async XLA Ops:
  1.3 23.4 %copy-start = (f32[8,1024]{1,0:T(8,128)S(1)}, f32[8,1024]{1,0:T(8,128)}, u32[]{:S(2)}) copy-start(f32[8,1024]{1,0:T(8,128)} %param.11) | copy-start | bytes 98308
  24.7 1.4 %copy-start.1 = (f32[8,1024]{1,0:T(8,128)S(1)}, f32[8,1024]{1,0:T(8,128)}, u32[]{:S(2)}) copy-start(f32[8,1024]{1,0:T(8,128)} %residual_in.1) | copy-start | bytes 98308
  24.7 1.4 %copy-start.2 = (f32[8,1024]{1,0:T(8,128)S(1)}, f32[8,1024]{1,0:T(8,128)}, u32[]{:S(2)}) copy-start(f32[8,1024]{1,0:T(8,128)} %get-tuple-element.7) | copy-start | bytes 98308
  24.7 1.4 %copy-start.3 = (f32[8,1024]{1,0:T(8,128)S(1)}, f32[8,1024]{1,0:T(8,128)}, u32[]{:S(2)}) copy-start(f32[8,1024]{1,0:T(8,128)} %get-tuple-element.8) | copy-start | bytes 98308

commit v4 on v3

--- a/solution.py
+++ b/solution.py
@@ -15,6 +15,14 @@
 DEPTH = 64
 
 
+def spread(col, nc):
+    return (col % 2) * (nc // 2) + col // 2
+
+
+def gather_place(quarter, nc):
+    return (quarter % (nc // 2)) * 2 + quarter // (nc // 2)
+
+
 def split3(x):
     first = x.astype(jnp.bfloat16).astype(jnp.float32)
     second = (x - first).astype(jnp.bfloat16).astype(jnp.float32)
@@ -33,7 +41,7 @@
 def kernel(
     nb, nc, tile,
     points_in, lengths_in, noise_in, outscale_in, residual_in, direction_in,
-    step_out, drop_out, keep_out,
+    changes,
     points, lengths, noise, outscale, residual, direction, in_sems,
     low_own, pts_own, low_buf, pts_buf, far, near, low_all, kmat_a, kmat_b, part, part_in, stat, stat_in,
     low_send, low_recv, pts_send, pts_recv, part_send, part_recv, stat_send, stat_recv,
@@ -45,9 +53,10 @@
     cols = direction.shape[0]
     half = count // 2
     tiles = count // tile
-    quarter = b // per
+    keeper = gather_place(b // per, nc)
+    base = spread(c, nc) * per
     slot = b % per
-    mine = quarter == c
+    mine = keeper == c
 
     loads = [
         pltpu.make_async_copy(source, target, in_sems.at[index])
@@ -67,7 +76,7 @@
         pl.semaphore_signal(barrier, inc=1, device_id=(block, col), device_id_type=MESH)
 
     def greet_sources(k, carry):
-        block = c * per + k // nc
+        block = base + k // nc
         col = k % nc
 
         @pl.when(jnp.logical_or(block != b, col != c))
@@ -105,14 +114,14 @@
         return pltpu.make_async_remote_copy(
             src_ref=pts_own, dst_ref=pts_buf.at[slot],
             send_sem=pts_send.at[k], recv_sem=pts_recv.at[slot],
-            device_id=(k, quarter), device_id_type=MESH,
+            device_id=(k, keeper), device_id_type=MESH,
         )
 
     def low_copy(k):
         return pltpu.make_async_remote_copy(
             src_ref=low_own, dst_ref=low_buf.at[slot, c],
             send_sem=low_send.at[k], recv_sem=low_recv.at[slot, c],
-            device_id=(k, quarter), device_id_type=MESH,
+            device_id=(k, keeper), device_id_type=MESH,
         )
 
     def each_pts(act):
@@ -157,7 +166,7 @@
     shift = jnp.log(outscale[...] * (LN2 * LN2 / 3.0)) * LOG2E
 
     def form(jb):
-        @pl.when(c * per + jb != b)
+        @pl.when(base + jb != b)
         def _():
             pltpu.make_async_copy(pts_buf.at[jb], pts_buf.at[jb], pts_recv.at[jb]).wait()
 
@@ -179,7 +188,7 @@
 
     def wait_low(jb):
         for col in range(nc):
-            @pl.when(jnp.logical_or(c * per + jb != b, c != col))
+            @pl.when(jnp.logical_or(base + jb != b, c != col))
             def _():
                 pltpu.make_async_copy(
                     low_buf.at[jb, col], low_buf.at[jb, col], low_recv.at[jb, col]
@@ -271,9 +280,9 @@
     curve, mixed, power, norm_now = (sums[:, index : index + 1] for index in range(4))
     alpha = norm_now / curve
     norm_next = norm_now - 2.0 * alpha * mixed + alpha * alpha * power
-    step_out[...] = alpha * own
-    drop_out[...] = alpha * image
-    keep_out[...] = (norm_next / norm_now) * own
+    changes[0:cols] = alpha * own
+    changes[cols : 2 * cols] = alpha * image
+    changes[2 * cols : 3 * cols] = (norm_next / norm_now) * own
 
     each_pts(lambda copy: copy.wait_send())
     each_low(lambda copy: copy.wait_send())
@@ -298,15 +307,14 @@
     tile = math.gcd(count, 256)
     tiles = count // tile
     vmem = pl.BlockSpec(memory_space=pltpu.VMEM)
-    state = jax.ShapeDtypeStruct((cols, count), jnp.float32)
     here = pl.BlockSpec(memory_space=pl.ANY)
     dma = pltpu.SemaphoreType.DMA
     entries = per * count * count
-    step, drop, keep = pl.pallas_call(
+    changes = pl.pallas_call(
         functools.partial(kernel, nb, nc, tile),
-        out_shape=(state, state, state),
+        out_shape=jax.ShapeDtypeStruct((3 * cols, count), jnp.float32),
         in_specs=[here] * 6,
-        out_specs=(vmem, vmem, vmem),
+        out_specs=vmem,
         scratch_shapes=[
             pltpu.VMEM((dim, count), jnp.float32),
             pltpu.SMEM((dim,), jnp.float32),
@@ -338,8 +346,8 @@
             flops=2 * entries * (DEPTH + nc * cols), bytes_accessed=1 << 19, transcendentals=2 * entries
         ),
     )(points, lengths, noise.reshape(1, count), outscale.reshape(1, 1), residual, direction)
-    after = residual - drop
-    return (solution + step, after, after + keep)
+    after = residual - changes[cols : 2 * cols]
+    return (solution + changes[:cols], after, after + changes[2 * cols :])
 
 
 def solution(mesh):

time: 27 us -> 28.4 us (1.052)
  Pallas kernels: 23.4 us -> 25.4 us
  other arithmetic: 2.03 us -> 1.44 us
    pallas_call x1, Pallas kernels: 23.4 us -> 25.4 us  [local(): pl.pallas_call(functools.partial(kernel, nb, nc, tile), out_shape=jax.Sha...]
    add x2 -> x1, other arithmetic: 2.03 us -> 1.44 us  [local(): return (solution + changes[:cols], after, after + changes[2 * cols:])]
where the time goes in v4:
time: 28.4 us; the launch traced here: 28.1 us
  Pallas kernels  25.4 us (89%)
  other arithmetic  1.44 us (5%)
  between operations  1.32 us (5%)
    pallas_call x1, Pallas kernels, local(): pl.pallas_call(functools.partial(kernel, nb, nc, tile), out_shape=jax.Sha...  25.4 us
    add x1, other arithmetic, local(): return (solution + changes[:cols], after, after + changes[2 * cols:])  1.44 us

profile of v4, /device:TPU:0, one launch (start us, length us, event | category | flops | bytes accessed | tf_op | source)
XLA Modules:
  0.0 28.1 jit_solution(7430122761630665834)
XLA Ops:
  1.3 0.0 copy-start
  1.3 0.0 copy-start.1
  1.3 25.4 %shard_map.94 = f32[24,1024]{1,0:T(8,128)} custom-call(f32[16,1024]{1,0:T(8,128)} %points_in.1, f32[16]{0:T(128)} %lengths_in.1, f32[1,1024]{1,0:T(1,128)} %bitcast.3, f32[1,1]{1,0:T(1,128)} %bitcast.2.outscale_in, f32[8,1024]{1,0:T(8,128)} %residual_in.1, f32[8,1024]{1,0:T(8,128)} %direction_in.1), custom_call_target="tpu_custom_call" | custom-call | flops 402653184 | bytes 524288 | tf_op jit(solution)/shard_map/pallas_call | solution.py:313
  26.7 0.0 copy-done
  26.7 0.0 copy-done.1
  26.7 1.4 %slice_add_fusion = (f32[8,1024]{1,0:T(8,128)}, f32[8,1024]{1,0:T(8,128)}, f32[8,1024]{1,0:T(8,128)}) fusion(f32[24,1024]{1,0:T(8,128)} %shard_map.94, f32[8,1024]{1,0:T(8,128)S(1)} %copy-done, f32[8,1024]{1,0:T(8,128)S(1)} %copy-done.1), kind=kLoop, calls=%fused_computation | loop fusion | flops 24576 | bytes 262144 | tf_op jit(solution)/shard_map/add | solution.py:350
Async XLA Ops:
  1.3 25.4 %copy-start = (f32[8,1024]{1,0:T(8,128)S(1)}, f32[8,1024]{1,0:T(8,128)}, u32[]{:S(2)}) copy-start(f32[8,1024]{1,0:T(8,128)} %residual_in.1) | copy-start | bytes 98308
  1.3 25.4 %copy-start.1 = (f32[8,1024]{1,0:T(8,128)S(1)}, f32[8,1024]{1,0:T(8,128)}, u32[]{:S(2)}) copy-start(f32[8,1024]{1,0:T(8,128)} %param.11) | copy-start | bytes 98308

commit v5 on v4

--- a/solution.py
+++ b/solution.py
@@ -13,14 +13,6 @@
 LN2 = math.log(2.0)
 KAPPA = 5.0 * LOG2E * LOG2E
 DEPTH = 64
-
-
-def spread(col, nc):
-    return (col % 2) * (nc // 2) + col // 2
-
-
-def gather_place(quarter, nc):
-    return (quarter % (nc // 2)) * 2 + quarter // (nc // 2)
 
 
 def split3(x):
@@ -53,8 +45,8 @@
     cols = direction.shape[0]
     half = count // 2
     tiles = count // tile
-    keeper = gather_place(b // per, nc)
-    base = spread(c, nc) * per
+    keeper = b // per
+    base = c * per
     slot = b % per
     mine = keeper == c
 
@@ -178,13 +170,18 @@
         )
         far[...] = stacked.T
 
+    piece = math.gcd(count, 64)
+
     def fill(it, kmat):
         cut = slice(it * tile, (it + 1) * tile)
-        gap = jnp.dot(far[...], near[:, cut], preferred_element_type=jnp.float32)
-        gap = jnp.maximum(gap, 1e-30)
-        radius = gap * lax.rsqrt(gap)
-        value = ((radius + 3.0 / LN2) * radius + 3.0 / (LN2 * LN2)) * jnp.exp2(shift - radius)
-        kmat[:, cut] = value.astype(jnp.bfloat16)
+        for start in range(0, count, piece):
+            gap = jnp.dot(
+                far[start : start + piece], near[:, cut], preferred_element_type=jnp.float32
+            )
+            gap = jnp.maximum(gap, 1e-30)
+            radius = gap * lax.rsqrt(gap)
+            value = ((radius + 3.0 / LN2) * radius + 3.0 / (LN2 * LN2)) * jnp.exp2(shift - radius)
+            kmat[start : start + piece, cut] = value.astype(jnp.bfloat16)
 
     def wait_low(jb):
         for col in range(nc):

time: 28.4 us -> 26.7 us (0.940)
  Pallas kernels: 25.4 us -> 23.7 us
    pallas_call x1, Pallas kernels: 25.4 us -> 23.7 us  [local(): pl.pallas_call(functools.partial(kernel, nb, nc, tile), out_shape=jax.Sha...]
where the time goes in v5:
time: 26.7 us; the launch traced here: 26.5 us
  Pallas kernels  23.7 us (89%)
  other arithmetic  1.44 us (5%)
  between operations  1.32 us (5%)
    pallas_call x1, Pallas kernels, local(): pl.pallas_call(functools.partial(kernel, nb, nc, tile), out_shape=jax.Sha...  23.7 us
    add x1, other arithmetic, local(): return (solution + changes[:cols], after, after + changes[2 * cols:])  1.44 us

profile of v5, /device:TPU:0, one launch (start us, length us, event | category | flops | bytes accessed | tf_op | source)
XLA Modules:
  0.0 26.5 jit_solution(13142096916475500849)
XLA Ops:
  1.3 0.0 copy-start
  1.3 0.0 copy-start.1
  1.3 23.7 %shard_map.94 = f32[24,1024]{1,0:T(8,128)} custom-call(f32[16,1024]{1,0:T(8,128)} %points_in.1, f32[16]{0:T(128)} %lengths_in.1, f32[1,1024]{1,0:T(1,128)} %bitcast.3, f32[1,1]{1,0:T(1,128)} %bitcast.2.outscale_in, f32[8,1024]{1,0:T(8,128)} %residual_in.1, f32[8,1024]{1,0:T(8,128)} %direction_in.1), custom_call_target="tpu_custom_call" | custom-call | flops 402653184 | bytes 524288 | tf_op jit(solution)/shard_map/pallas_call | solution.py:310
  25.0 0.0 copy-done
  25.0 0.0 copy-done.1
  25.0 1.4 %slice_add_fusion = (f32[8,1024]{1,0:T(8,128)}, f32[8,1024]{1,0:T(8,128)}, f32[8,1024]{1,0:T(8,128)}) fusion(f32[24,1024]{1,0:T(8,128)} %shard_map.94, f32[8,1024]{1,0:T(8,128)S(1)} %copy-done, f32[8,1024]{1,0:T(8,128)S(1)} %copy-done.1), kind=kLoop, calls=%fused_computation | loop fusion | flops 24576 | bytes 262144 | tf_op jit(solution)/shard_map/add | solution.py:347
Async XLA Ops:
  1.3 23.7 %copy-start = (f32[8,1024]{1,0:T(8,128)S(1)}, f32[8,1024]{1,0:T(8,128)}, u32[]{:S(2)}) copy-start(f32[8,1024]{1,0:T(8,128)} %residual_in.1) | copy-start | bytes 98308
  1.3 23.7 %copy-start.1 = (f32[8,1024]{1,0:T(8,128)S(1)}, f32[8,1024]{1,0:T(8,128)}, u32[]{:S(2)}) copy-start(f32[8,1024]{1,0:T(8,128)} %param.11) | copy-start | bytes 98308

commit v6 on v5

--- a/solution.py
+++ b/solution.py
@@ -20,6 +20,14 @@
     second = (x - first).astype(jnp.bfloat16).astype(jnp.float32)
     third = x - first - second
     return first, second, third
+
+
+def repeat(low, high, step):
+    if high - low <= 8:
+        for index in range(low, high):
+            step(index, 0)
+    else:
+        lax.fori_loop(low, high, step, 0)
 
 
 def extra_rows(rows, count):
@@ -59,9 +67,6 @@
             )
         )
     ]
-    for load in loads:
-        load.start()
-
     barrier = pltpu.get_barrier_semaphore()
 
     def greet(block, col):
@@ -77,15 +82,12 @@
 
         return carry
 
-    lax.fori_loop(0, per * nc, greet_sources, 0)
-
-    def greet_blocks(k, carry):
-        greet((b + k) % nb, c)
-        return carry
-
-    lax.fori_loop(1, nb, greet_blocks, 0)
+    repeat(0, per * nc, greet_sources)
+
     for k in range(1, nc):
         greet(b, (c + k) % nc)
+    for load in loads:
+        load.start()
 
     for load in loads:
         load.wait()
@@ -99,7 +101,7 @@
     low_own[...] = jnp.concatenate([own[:, :half], own[:, half:]], axis=0).astype(jnp.bfloat16)
 
     pl.semaphore_wait(
-        barrier, nb - jnp.where(mine, 1, 0) + nb - 1 + nc - 1
+        barrier, nb - jnp.where(mine, 1, 0) + nc - 1
     )
 
     def pts_copy(k):
@@ -126,7 +128,7 @@
 
             return carry
 
-        lax.fori_loop(0, per, step, 0)
+        repeat(0, per, step)
 
     def each_low(act):
         def step(k, carry):
@@ -138,7 +140,7 @@
 
             return carry
 
-        lax.fori_loop(0, nb, step, 0)
+        repeat(0, nb, step)
 
     each_pts(lambda copy: copy.start())
     each_low(lambda copy: copy.start())
@@ -224,29 +226,28 @@
     if per > 2:
         lax.fori_loop(1, per // 2, pair, 0)
 
-    def part_copy(it, col):
-        cut = pl.ds(pl.multiple_of(it * tile, tile), tile)
+    def part_copy(col, start, width):
+        cut = pl.ds(start, width)
         return pltpu.make_async_remote_copy(
             src_ref=part.at[col, :, cut], dst_ref=part_in.at[c, :, cut],
-            send_sem=part_send.at[it, col], recv_sem=part_recv.at[it, c],
+            send_sem=part_send.at[col], recv_sem=part_recv.at[c],
             device_id=(b, col), device_id_type=MESH,
         )
 
     wait_low(per - 1)
     for it in range(tiles):
         add_image(it, kmat_b, False)
-        for k in range(1, nc):
-            part_copy(it, (c + k) % nc).start()
-
+        if it % 2 == 1:
+            for k in range(1, nc):
+                part_copy((c + k) % nc, (it - 1) * tile, 2 * tile).start()
+
+    each_pts(lambda copy: copy.wait_send())
+    each_low(lambda copy: copy.wait_send())
     now = residual[...]
     image = part[c] + noise[...] * own
     for k in range(1, nc):
         col = (c + k) % nc
-        for it in range(tiles):
-            cut = pl.ds(it * tile, tile)
-            pltpu.make_async_copy(
-                part_in.at[col, :, cut], part_in.at[col, :, cut], part_recv.at[it, col]
-            ).wait()
+        pltpu.make_async_copy(part_in.at[col], part_in.at[col], part_recv.at[col]).wait()
         image = image + part_in[col]
 
     lane = lax.broadcasted_iota(jnp.int32, (cols, 128), 1)
@@ -266,7 +267,10 @@
         stat_copy((b + k) % nb).start()
         return carry
 
-    lax.fori_loop(1, nb, start_stat, 0)
+    repeat(1, nb, start_stat)
+
+    for k in range(1, nc):
+        part_copy((c + k) % nc, 0, count).wait_send()
 
     def add_stat(k, total):
         block = (b + k) % nb
@@ -281,20 +285,11 @@
     changes[cols : 2 * cols] = alpha * image
     changes[2 * cols : 3 * cols] = (norm_next / norm_now) * own
 
-    each_pts(lambda copy: copy.wait_send())
-    each_low(lambda copy: copy.wait_send())
-
-    def sent_part(k, carry):
-        part_copy(k // (nc - 1), (c + 1 + k % (nc - 1)) % nc).wait_send()
-        return carry
-
-    lax.fori_loop(0, tiles * (nc - 1), sent_part, 0)
-
     def sent_stat(k, carry):
         stat_copy((b + k) % nb).wait_send()
         return carry
 
-    lax.fori_loop(1, nb, sent_stat, 0)
+    repeat(1, nb, sent_stat)
 
 
 def local(nb, nc, points, lengths, noise, outscale, solution, residual, direction):
@@ -334,7 +329,7 @@
             pltpu.VMEM((cols, 128), jnp.float32),
             pltpu.VMEM((nb, cols, 128), jnp.float32),
             dma((nb,)), dma((per, nc)), dma((nb,)), dma((per,)),
-            dma((tiles, nc)), dma((tiles, nc)), dma((nb,)), dma((nb,)),
+            dma((nc,)), dma((nc,)), dma((nb,)), dma((nb,)),
         ],
         compiler_params=pltpu.CompilerParams(
             collective_id=0, has_side_effects=True, vmem_limit_bytes=56 * 1024 * 1024

time: 26.7 us -> 25.7 us (0.963)
  Pallas kernels: 23.7 us -> 22.7 us
    pallas_call x1, Pallas kernels: 23.7 us -> 22.7 us  [local(): pl.pallas_call(functools.partial(kernel, nb, nc, tile), out_shape=jax.Sha...]
where the time goes in v6:
time: 25.7 us; the launch traced here: 25.5 us
  Pallas kernels  22.7 us (88%)
  other arithmetic  1.44 us (6%)
  between operations  1.32 us (5%)
    pallas_call x1, Pallas kernels, local(): pl.pallas_call(functools.partial(kernel, nb, nc, tile), out_shape=jax.Sha...  22.7 us
    add x1, other arithmetic, local(): return (solution + changes[:cols], after, after + changes[2 * cols:])  1.44 us

profile of v6, /device:TPU:0, one launch (start us, length us, event | category | flops | bytes accessed | tf_op | source)
XLA Modules:
  0.0 25.5 jit_solution(17266168989750666009)
XLA Ops:
  1.3 0.0 copy-start
  1.3 0.0 copy-start.1
  1.3 22.7 %shard_map.94 = f32[24,1024]{1,0:T(8,128)} custom-call(f32[16,1024]{1,0:T(8,128)} %points_in.1, f32[16]{0:T(128)} %lengths_in.1, f32[1,1024]{1,0:T(1,128)} %bitcast.3, f32[1,1]{1,0:T(1,128)} %bitcast.2.outscale_in, f32[8,1024]{1,0:T(8,128)} %residual_in.1, f32[8,1024]{1,0:T(8,128)} %direction_in.1), custom_call_target="tpu_custom_call" | custom-call | flops 402653184 | bytes 524288 | tf_op jit(solution)/shard_map/pallas_call | solution.py:305
  24.0 0.0 copy-done
  24.0 0.0 copy-done.1
  24.0 1.4 %slice_add_fusion = (f32[8,1024]{1,0:T(8,128)}, f32[8,1024]{1,0:T(8,128)}, f32[8,1024]{1,0:T(8,128)}) fusion(f32[24,1024]{1,0:T(8,128)} %shard_map.94, f32[8,1024]{1,0:T(8,128)S(1)} %copy-done, f32[8,1024]{1,0:T(8,128)S(1)} %copy-done.1), kind=kLoop, calls=%fused_computation | loop fusion | flops 24576 | bytes 262144 | tf_op jit(solution)/shard_map/add | solution.py:342
Async XLA Ops:
  1.3 22.7 %copy-start = (f32[8,1024]{1,0:T(8,128)S(1)}, f32[8,1024]{1,0:T(8,128)}, u32[]{:S(2)}) copy-start(f32[8,1024]{1,0:T(8,128)} %residual_in.1) | copy-start | bytes 98308
  1.3 22.7 %copy-start.1 = (f32[8,1024]{1,0:T(8,128)S(1)}, f32[8,1024]{1,0:T(8,128)}, u32[]{:S(2)}) copy-start(f32[8,1024]{1,0:T(8,128)} %param.11) | copy-start | bytes 98308

commit v7 on v6

--- a/solution.py
+++ b/solution.py
@@ -143,7 +143,6 @@
         repeat(0, nb, step)
 
     each_pts(lambda copy: copy.start())
-    each_low(lambda copy: copy.start())
 
     @pl.when(mine)
     def _():
@@ -159,11 +158,12 @@
 
     shift = jnp.log(outscale[...] * (LN2 * LN2 / 3.0)) * LOG2E
 
-    def form(jb):
+    def wait_pts(jb):
         @pl.when(base + jb != b)
         def _():
             pltpu.make_async_copy(pts_buf.at[jb], pts_buf.at[jb], pts_recv.at[jb]).wait()
 
+    def form(jb):
         other = pts_buf[jb]
         wide = other.astype(jnp.float32)
         squares = split3(KAPPA * jnp.sum(wide * wide, axis=0, keepdims=True))
@@ -207,12 +207,15 @@
             part[col, :, cut] = rows if first else part[col, :, cut] + rows
 
     def both(jb, now_mat, last_mat, first):
+        wait_pts(jb)
         form(jb)
         wait_low(jb - 1)
         for it in range(tiles):
             fill(it, now_mat)
             add_image(it, last_mat, first)
 
+    wait_pts(0)
+    each_low(lambda copy: copy.start())
     form(0)
     for it in range(tiles):
         fill(it, kmat_a)

time: 25.7 us -> 28.4 us (1.11)
  Pallas kernels: 22.7 us -> 25.4 us
    pallas_call x1, Pallas kernels: 22.7 us -> 25.4 us  [local(): pl.pallas_call(functools.partial(kernel, nb, nc, tile), out_shape=jax.Sha...]
where the time goes in v7:
time: 28.4 us; the launch traced here: 28.2 us
  Pallas kernels  25.4 us (89%)
  other arithmetic  1.44 us (5%)
  between operations  1.32 us (5%)
    pallas_call x1, Pallas kernels, local(): pl.pallas_call(functools.partial(kernel, nb, nc, tile), out_shape=jax.Sha...  25.4 us
    add x1, other arithmetic, local(): return (solution + changes[:cols], after, after + changes[2 * cols:])  1.44 us

profile of v7, /device:TPU:0, one launch (start us, length us, event | category | flops | bytes accessed | tf_op | source)
XLA Modules:
  0.0 28.2 jit_solution(11088704268486584140)
XLA Ops:
  1.3 0.0 copy-start
  1.3 0.0 copy-start.1
  1.3 25.4 %shard_map.94 = f32[24,1024]{1,0:T(8,128)} custom-call(f32[16,1024]{1,0:T(8,128)} %points_in.1, f32[16]{0:T(128)} %lengths_in.1, f32[1,1024]{1,0:T(1,128)} %bitcast.3, f32[1,1]{1,0:T(1,128)} %bitcast.2.outscale_in, f32[8,1024]{1,0:T(8,128)} %residual_in.1, f32[8,1024]{1,0:T(8,128)} %direction_in.1), custom_call_target="tpu_custom_call" | custom-call | flops 402653184 | bytes 524288 | tf_op jit(solution)/shard_map/pallas_call | solution.py:308
  26.7 0.0 copy-done
  26.7 0.0 copy-done.1
  26.8 1.4 %slice_add_fusion = (f32[8,1024]{1,0:T(8,128)}, f32[8,1024]{1,0:T(8,128)}, f32[8,1024]{1,0:T(8,128)}) fusion(f32[24,1024]{1,0:T(8,128)} %shard_map.94, f32[8,1024]{1,0:T(8,128)S(1)} %copy-done, f32[8,1024]{1,0:T(8,128)S(1)} %copy-done.1), kind=kLoop, calls=%fused_computation | loop fusion | flops 24576 | bytes 262144 | tf_op jit(solution)/shard_map/add | solution.py:345
Async XLA Ops:
  1.3 25.5 %copy-start = (f32[8,1024]{1,0:T(8,128)S(1)}, f32[8,1024]{1,0:T(8,128)}, u32[]{:S(2)}) copy-start(f32[8,1024]{1,0:T(8,128)} %residual_in.1) | copy-start | bytes 98308
  1.3 25.5 %copy-start.1 = (f32[8,1024]{1,0:T(8,128)S(1)}, f32[8,1024]{1,0:T(8,128)}, u32[]{:S(2)}) copy-start(f32[8,1024]{1,0:T(8,128)} %param.11) | copy-start | bytes 98308

commit v8 on v6

--- a/solution.py
+++ b/solution.py
@@ -185,7 +185,7 @@
             value = ((radius + 3.0 / LN2) * radius + 3.0 / (LN2 * LN2)) * jnp.exp2(shift - radius)
             kmat[start : start + piece, cut] = value.astype(jnp.bfloat16)
 
-    def wait_low(jb):
+    def wait_low(jb, place):
         for col in range(nc):
             @pl.when(jnp.logical_or(base + jb != b, c != col))
             def _():
@@ -197,33 +197,32 @@
         for col in range(nc):
             wide = low_buf[jb, col].astype(jnp.float32)
             shards.append(jnp.concatenate([wide[:cols], wide[cols:]], axis=1))
-        low_all[...] = jnp.concatenate(shards, axis=0).astype(jnp.bfloat16)
-
-    def add_image(it, kmat, first):
+        low_all[place] = jnp.concatenate(shards, axis=0).astype(jnp.bfloat16)
+
+    def add_image(it, kmat, place, first):
         cut = slice(it * tile, (it + 1) * tile)
-        total = jnp.dot(low_all[...], kmat[:, cut], preferred_element_type=jnp.float32)
+        total = jnp.dot(low_all[place], kmat[:, cut], preferred_element_type=jnp.float32)
         for col in range(nc):
             rows = total[col * cols : (col + 1) * cols]
             part[col, :, cut] = rows if first else part[col, :, cut] + rows
 
-    def both(jb, now_mat, last_mat, first):
-        form(jb)
-        wait_low(jb - 1)
+    mats = (kmat_a, kmat_b)
+    for slot_index in range(2):
+        form(slot_index)
         for it in range(tiles):
-            fill(it, now_mat)
-            add_image(it, last_mat, first)
-
-    form(0)
-    for it in range(tiles):
-        fill(it, kmat_a)
-    both(1, kmat_b, kmat_a, True)
+            fill(it, mats[slot_index])
 
     def pair(p, carry):
-        both(2 * p, kmat_a, kmat_b, False)
-        both(2 * p + 1, kmat_b, kmat_a, False)
+        for index in range(2):
+            wait_low(2 * p - 2 + index, index)
+            form(2 * p + index)
+            for it in range(tiles):
+                add_image(it, mats[index], index, False)
+                fill(it, mats[index])
         return carry
 
     if per > 2:
+        part[...] = jnp.zeros_like(part)
         lax.fori_loop(1, per // 2, pair, 0)
 
     def part_copy(col, start, width):
@@ -234,9 +233,11 @@
             device_id=(b, col), device_id_type=MESH,
         )
 
-    wait_low(per - 1)
+    for index in range(2):
+        wait_low(per - 2 + index, index)
     for it in range(tiles):
-        add_image(it, kmat_b, False)
+        for index in range(2):
+            add_image(it, mats[index], index, per == 2 and index == 0)
         if it % 2 == 1:
             for k in range(1, nc):
                 part_copy((c + k) % nc, (it - 1) * tile, 2 * tile).start()
@@ -321,7 +322,7 @@
             pltpu.VMEM((per, dim, count), jnp.bfloat16),
             pltpu.VMEM((count, DEPTH), jnp.bfloat16),
             pltpu.VMEM((DEPTH, count), jnp.bfloat16),
-            pltpu.VMEM((nc * cols, count), jnp.bfloat16),
+            pltpu.VMEM((2, nc * cols, count), jnp.bfloat16),
             pltpu.VMEM((count, count), jnp.bfloat16),
             pltpu.VMEM((count, count), jnp.bfloat16),
             pltpu.VMEM((nc, cols, count), jnp.float32),

time: 25.7 us -> 25.7 us (level)
  no operation moved by 1% of the time
where the time goes in v8:
time: 25.7 us; the launch traced here: 25.5 us
  Pallas kernels  22.7 us (88%)
  other arithmetic  1.44 us (6%)
  between operations  1.32 us (5%)
    pallas_call x1, Pallas kernels, local(): pl.pallas_call(functools.partial(kernel, nb, nc, tile), out_shape=jax.Sha...  22.7 us
    add x1, other arithmetic, local(): return (solution + changes[:cols], after, after + changes[2 * cols:])  1.44 us

profile of v8, /device:TPU:0, one launch (start us, length us, event | category | flops | bytes accessed | tf_op | source)
XLA Modules:
  0.0 25.5 jit_solution(11961785538269106829)
XLA Ops:
  1.3 0.0 copy-start
  1.3 0.0 copy-start.1
  1.3 22.7 %shard_map.94 = f32[24,1024]{1,0:T(8,128)} custom-call(f32[16,1024]{1,0:T(8,128)} %points_in.1, f32[16]{0:T(128)} %lengths_in.1, f32[1,1024]{1,0:T(1,128)} %bitcast.3, f32[1,1]{1,0:T(1,128)} %bitcast.2.outscale_in, f32[8,1024]{1,0:T(8,128)} %residual_in.1, f32[8,1024]{1,0:T(8,128)} %direction_in.1), custom_call_target="tpu_custom_call" | custom-call | flops 402653184 | bytes 524288 | tf_op jit(solution)/shard_map/pallas_call | solution.py:306
  24.0 0.0 copy-done
  24.0 0.0 copy-done.1
  24.1 1.4 %slice_add_fusion = (f32[8,1024]{1,0:T(8,128)}, f32[8,1024]{1,0:T(8,128)}, f32[8,1024]{1,0:T(8,128)}) fusion(f32[24,1024]{1,0:T(8,128)} %shard_map.94, f32[8,1024]{1,0:T(8,128)S(1)} %copy-done, f32[8,1024]{1,0:T(8,128)S(1)} %copy-done.1), kind=kLoop, calls=%fused_computation | loop fusion | flops 24576 | bytes 262144 | tf_op jit(solution)/shard_map/add | solution.py:343
Async XLA Ops:
  1.3 22.8 %copy-start = (f32[8,1024]{1,0:T(8,128)S(1)}, f32[8,1024]{1,0:T(8,128)}, u32[]{:S(2)}) copy-start(f32[8,1024]{1,0:T(8,128)} %residual_in.1) | copy-start | bytes 98308
  1.3 22.8 %copy-start.1 = (f32[8,1024]{1,0:T(8,128)S(1)}, f32[8,1024]{1,0:T(8,128)}, u32[]{:S(2)}) copy-start(f32[8,1024]{1,0:T(8,128)} %param.11) | copy-start | bytes 98308

commit v9 on v8

--- a/solution.py
+++ b/solution.py
@@ -130,11 +130,15 @@
 
         repeat(0, per, step)
 
+    half_blocks = nb // 2
+    side = b // half_blocks
+
     def each_low(act):
         def step(k, carry):
-            block = (b + k) % nb
-
-            @pl.when(jnp.logical_or(k != 0, jnp.logical_not(mine)))
+            other = lax.rem(side + 1 + k // half_blocks, 2)
+            block = other * half_blocks + (b + k) % half_blocks
+
+            @pl.when(jnp.logical_or(k != half_blocks, jnp.logical_not(mine)))
             def _():
                 act(low_copy(block))
 

time: 25.7 us -> 25.7 us (level)
  no operation moved by 1% of the time
where the time goes in v9:
time: 25.7 us; the launch traced here: 25.5 us
  Pallas kernels  22.7 us (88%)
  other arithmetic  1.44 us (6%)
  between operations  1.32 us (5%)
    pallas_call x1, Pallas kernels, local(): pl.pallas_call(functools.partial(kernel, nb, nc, tile), out_shape=jax.Sha...  22.7 us
    add x1, other arithmetic, local(): return (solution + changes[:cols], after, after + changes[2 * cols:])  1.44 us

profile of v9, /device:TPU:0, one launch (start us, length us, event | category | flops | bytes accessed | tf_op | source)
XLA Modules:
  0.0 25.5 jit_solution(6664533406285625690)
XLA Ops:
  1.3 0.0 copy-start
  1.3 0.0 copy-start.1
  1.3 22.7 %shard_map.94 = f32[24,1024]{1,0:T(8,128)} custom-call(f32[16,1024]{1,0:T(8,128)} %points_in.1, f32[16]{0:T(128)} %lengths_in.1, f32[1,1024]{1,0:T(1,128)} %bitcast.3, f32[1,1]{1,0:T(1,128)} %bitcast.2.outscale_in, f32[8,1024]{1,0:T(8,128)} %residual_in.1, f32[8,1024]{1,0:T(8,128)} %direction_in.1), custom_call_target="tpu_custom_call" | custom-call | flops 402653184 | bytes 524288 | tf_op jit(solution)/shard_map/pallas_call | solution.py:310
  24.0 0.0 copy-done
  24.0 0.0 copy-done.1
  24.1 1.4 %slice_add_fusion = (f32[8,1024]{1,0:T(8,128)}, f32[8,1024]{1,0:T(8,128)}, f32[8,1024]{1,0:T(8,128)}) fusion(f32[24,1024]{1,0:T(8,128)} %shard_map.94, f32[8,1024]{1,0:T(8,128)S(1)} %copy-done, f32[8,1024]{1,0:T(8,128)S(1)} %copy-done.1), kind=kLoop, calls=%fused_computation | loop fusion | flops 24576 | bytes 262144 | tf_op jit(solution)/shard_map/add | solution.py:347
Async XLA Ops:
  1.3 22.8 %copy-start = (f32[8,1024]{1,0:T(8,128)S(1)}, f32[8,1024]{1,0:T(8,128)}, u32[]{:S(2)}) copy-start(f32[8,1024]{1,0:T(8,128)} %residual_in.1) | copy-start | bytes 98308
  1.3 22.8 %copy-start.1 = (f32[8,1024]{1,0:T(8,128)S(1)}, f32[8,1024]{1,0:T(8,128)}, u32[]{:S(2)}) copy-start(f32[8,1024]{1,0:T(8,128)} %param.11) | copy-start | bytes 98308
